TPU v7x, 32 devices: a whole 2x2x4 slice. The times are simulated.
32 devices in a mesh: groups: 2 (over y), bond: 4 (over z), mpo: 2 (over x), phys: 2 (over core).
Axes of the slice: x: 2, y: 2, z: 4, core: 2. Of those that a mesh axis runs over, the one named last changes fastest.
Arguments:
- psi: bfloat16 [256, 4, 128, 128], P(('groups', 'bond', 'phys')), parts along dimension 0, may hold values from -6 to 6
- left_env: bfloat16 [4, 16, 128, 128], P('mpo', ('groups', 'bond')), parts along dimension 1, may hold values from -0.5 to 0.5
- right_env: bfloat16 [4, 32, 128, 128], P('mpo', ('groups', 'bond')), parts along dimension 1, may hold values from -0.5 to 0.5
- mpo_ops: float32 [4, 4, 4], P('mpo'), may hold values from -3 to 3
- mpo_pattern: int32 [4, 4, 4], P('mpo'), may hold values 0 or 1
- left_mask: int32 [4, 16], P('mpo', 'groups'), parts along dimension 1, may hold values 0 or 1
- right_mask: int32 [4, 32], P('mpo', 'groups'), parts along dimension 1, may hold values 0 or 1
- left_sector: int32 [256], P('groups'), parts along dimension 0, may hold values from 0 to 7, as said below
- right_sector: int32 [256], P('groups'), parts along dimension 0, may hold values from 0 to 15, as said below
- left_size: int32 [16], P('groups'), parts along dimension 0, may hold values from 64 to 128
- right_size: int32 [32], P('groups'), parts along dimension 0, may hold values from 64 to 128
Outputs:
- h_psi: bfloat16 [256, 4, 128, 128], P(('groups', 'bond', 'phys'), None, 'mpo'), parts along dimension 0
There are 2 independent parts, one for each index of `groups`. A program takes and returns all parts, laid end to end along the dimension named above; an argument that names none is the same for every part. Nothing has to cross between parts.
Inputs may be any that keep to these rules, and one draw needn't show every extreme that they name: `left_sector`: blocks are ordered by device: index i of bond holds one aligned run of blocks, 16 on each index of phys in turn, and every block of that run has a left sector from i * 2 to i * 2 + 1. `right_sector`: the owner of right sector r is index r // 4 of bond. Within each aligned run of 16 blocks no owner is named by more than 4 blocks, and one owner is named exactly 4 times in every run.
All inputs are finite; a program needn't handle non-finite values. No bound on the sum of `mpo_pattern` or of `left_mask` or of `right_mask` on one device may be relied on, other than what follows from the above.
Results may differ from a plain program's by a relative error of at most 0.0095.
Values may be sent and summed in bfloat16 or wider, within the bound.
A program may use at most 64 MiB of HBM per device.

v0:
```python
import jax
import jax.numpy as jnp
from jax import lax
from jax.sharding import PartitionSpec as P


def copy_ranks(owner_rows):
    count = owner_rows.shape[-1]
    same = owner_rows[..., :, None] == owner_rows[..., None, :]
    earlier = jnp.arange(count)[None, :] < jnp.arange(count)[:, None]
    return jnp.sum(jnp.logical_and(same, earlier), axis=-1)


def shards(
    psi,
    left_env,
    right_env,
    mpo_ops,
    mpo_pattern,
    left_mask,
    right_mask,
    left_sector,
    right_sector,
    left_size,
    right_size,
):
    blocks, states, width, _ = psi.shape
    terms = left_env.shape[0]
    left_count = left_env.shape[1]
    right_count = right_env.shape[1]
    owners = lax.axis_size("bond")
    lane_slots = lax.axis_size("phys")
    copies = -(-blocks // owners)
    here = lax.axis_index("bond")
    lane = lax.axis_index("phys")
    right_lane = jnp.take(right_sector.reshape(owners, lane_slots, blocks), lane, axis=1)
    left_lane = jnp.take(left_sector.reshape(owners, lane_slots, blocks), lane, axis=1)
    mine_right = jnp.take(right_lane, here, axis=0)
    mine_left = jnp.take(left_lane, here, axis=0)
    positions = jnp.arange(width)
    left_dims = left_size[mine_left]
    col_keep = positions[None, :] < right_size[mine_right][:, None]
    row_keep = positions[None, :] < left_dims[:, None]
    keep = jnp.logical_and(row_keep[:, None, :, None], col_keep[:, None, None, :])
    masked = jnp.where(keep, psi, jnp.zeros((), jnp.bfloat16))
    local_left = mine_left - here * left_count
    operators = mpo_ops * mpo_pattern.astype(jnp.float32)
    weights = jnp.take(left_mask, mine_left, axis=1).astype(jnp.float32) * jnp.take(
        right_mask, mine_right, axis=1
    ).astype(jnp.float32)
    mixed_terms = []
    for term in range(terms):
        chosen = jnp.take(left_env[term], local_left, axis=0)
        product = jnp.einsum("jab,jsbc->jsac", chosen, masked, preferred_element_type=jnp.float32)
        combined = jnp.einsum(
            "st,jtac->jsac", operators[term], product, precision=lax.Precision.HIGHEST
        )
        mixed_terms.append((combined * weights[term][:, None, None, None]).astype(jnp.bfloat16))
    mixed = jnp.stack(mixed_terms, axis=1)
    part_rows = width // lax.axis_size("mpo")
    out_rows = lax.axis_index("mpo") * part_rows + jnp.arange(part_rows)
    out_keep = jnp.logical_and(
        (out_rows[None, :] < left_dims[:, None])[:, None, :, None], col_keep[:, None, None, :]
    )
    owner_all = right_lane // right_count
    rank_all = copy_ranks(owner_all)
    owner_mine = mine_right // right_count
    rank_mine = jnp.take(rank_all, here, axis=0)
    slot_ids = jnp.arange(owners * copies)
    hit = jnp.logical_and(
        owner_mine[None, :] == (slot_ids // copies)[:, None],
        rank_mine[None, :] == (slot_ids % copies)[:, None],
    )
    source = jnp.sum(jnp.where(hit, jnp.arange(blocks)[None, :], 0), axis=1)
    filled = jnp.any(hit, axis=1)
    outgoing = jnp.where(
        filled[:, None, None, None, None], mixed[source], jnp.zeros((), jnp.bfloat16)
    )
    incoming = lax.all_to_all(outgoing, "bond", split_axis=0, concat_axis=0, tiled=True)
    arrive = jnp.logical_and(
        owner_all[:, None, :] == here, rank_all[:, None, :] == jnp.arange(copies)[None, :, None]
    )
    which = jnp.sum(jnp.where(arrive, jnp.arange(blocks)[None, None, :], 0), axis=2)
    sector = jnp.take_along_axis(right_lane, which, axis=1).reshape(owners * copies)
    local_right = jnp.clip(sector - here * right_count, 0, right_count - 1)
    chosen_right = jnp.take(right_env, local_right, axis=1)
    partial_value = jnp.einsum(
        "nksab,knbc->nsac", incoming, chosen_right, preferred_element_type=jnp.float32
    ).astype(jnp.bfloat16)
    back_index = owner_mine * copies + rank_mine
    returned = lax.all_to_all(partial_value, "bond", split_axis=0, concat_axis=0, tiled=True)
    total = lax.psum_scatter(
        returned[back_index].astype(jnp.float32).astype(jnp.bfloat16),
        "mpo",
        scatter_dimension=2,
        tiled=True,
    ).astype(jnp.float32)
    return jnp.where(out_keep, total, 0.0).astype(jnp.bfloat16)


def solution(mesh):
    placed = (
        P(("groups", "bond", "phys"), None, None, None),
        P("mpo", ("groups", "bond"), None, None),
        P("mpo", ("groups", "bond"), None, None),
        P("mpo", None, None),
        P("mpo", None, None),
        P("mpo", "groups"),
        P("mpo", "groups"),
        P("groups"),
        P("groups"),
        P("groups"),
        P("groups"),
    )
    return jax.shard_map(
        shards,
        mesh=mesh,
        in_specs=placed,
        out_specs=P(("groups", "bond", "phys"), None, "mpo", None),
        check_vma=False,
    )
```

profile of v0, /device:TPU:0, one launch (start us, length us, event | category | flops | bytes accessed | tf_op | source)
XLA Modules:
  0.0 268.0 jit_solution(15851537675033252100)
XLA Ops:
  6.6 0.9 reshape.251
  7.5 0.2 convert_reduce_fusion
  7.7 0.2 select_reduce_fusion.1
  7.9 0.2 fusion.21
  8.1 0.8 copy.21
  8.9 0.7 reshape.250
  9.7 0.8 copy.20
  10.4 0.6 gather_fusion.3
  11.0 0.6 gather_fusion.2
  11.5 0.1 multiply_bitcast_fusion
  11.6 0.2 slice_reduce_fusion.1
  11.8 1.3 gather_fusion.1
  13.1 0.1 iota_compare_fusion.3
  13.2 1.3 gather_fusion
  14.5 0.1 iota_compare_fusion.1
  14.6 0.9 slice_bitcast_fusion.1
  15.5 0.3 broadcast_and_fusion
  15.9 0.6 gather_fusion.9
  16.5 0.0 copy-done.2
  16.5 2.8 %convolution_bitcast_fusion = f32[16,4,128,128]{2,3,1,0:T(8,128)} fusion(bf16[16,4,128,128]{3,2,1,0:T(8,128)(2,1)S(1)} %copy-done.2, pred[16,128,128]{2,1,0:T(8,128)(4,1)S(1)} %broadcast_and_fusion, bf16[16,128,128]{2,1,0:T(8,128)(2,1)S(1)} %gather_fusion.9, pred[16]{0:T(512)(128)(4,1)S(1)} %get-tuple-element.37), kind=kOutput, calls=%fused_computation.17 | convolution fusion | flops 269746176 | bytes 7077904 | tf_op jit(solution)/shard_map/jab,jsbc->jsac/dot_general | solution.py:54
  19.3 5.2 %copy.23 = f32[16,4,128,128]{3,1,2,0:T(4,128)} copy(f32[16,4,128,128]{2,3,1,0:T(8,128)} %convolution_bitcast_fusion) | data formatting | bytes 8388608 | tf_op jit(solution)/shard_map/jab,jsbc->jsac/transpose | solution.py:54
  24.6 0.6 gather_fusion.8
  25.2 2.8 %convolution_bitcast_fusion.1 = f32[16,4,128,128]{2,3,1,0:T(8,128)} fusion(bf16[16,4,128,128]{3,2,1,0:T(8,128)(2,1)S(1)} %copy-done.2, pred[16,128,128]{2,1,0:T(8,128)(4,1)S(1)} %broadcast_and_fusion, bf16[16,128,128]{2,1,0:T(8,128)(2,1)S(1)} %gather_fusion.8, pred[16]{0:T(512)(128)(4,1)S(1)} %get-tuple-element.37), kind=kOutput, calls=%fused_computation.18 | convolution fusion | flops 269746176 | bytes 7077904 | tf_op jit(solution)/shard_map/jab,jsbc->jsac/dot_general | solution.py:54
  28.1 5.3 %copy.19 = f32[16,4,128,128]{3,1,2,0:T(4,128)} copy(f32[16,4,128,128]{2,3,1,0:T(8,128)} %convolution_bitcast_fusion.1) | data formatting | bytes 8388608 | tf_op jit(solution)/shard_map/jab,jsbc->jsac/transpose | solution.py:54
  33.3 0.0 copy-done.4
  33.4 9.5 %fusion.5 = bf16[16,1,4,128,128]{4,2,3,0,1:T(4,128)(2,1)S(1)} fusion(f32[16]{0:T(128)S(1)} %get-tuple-element.31, f32[16,4,128,128]{3,1,2,0:T(4,128)} %copy.23, f32[2,4,4]{2,1,0:T(4,128)S(1)} %bitcast.96), kind=kOutput, calls=%fused_computation.22 | convolution fusion | flops 52428800 | bytes 6294016 | tf_op jit(solution)/shard_map/st,jtac->jsac/dot_general | solution.py:55
  42.9 8.0 %fusion.4 = bf16[16,1,4,128,128]{4,2,3,0,1:T(4,128)(2,1)S(1)} fusion(f32[16]{0:T(128)S(1)} %get-tuple-element.30, f32[16,4,128,128]{3,1,2,0:T(4,128)S(1)} %copy-done.1, f32[2,4,4]{2,1,0:T(4,128)S(1)} %bitcast.97), kind=kOutput, calls=%fused_computation.21 | convolution fusion | flops 52428800 | bytes 6294016 | tf_op jit(solution)/shard_map/st,jtac->jsac/dot_general | solution.py:55
  50.9 5.0 %pad_maximum_fusion = bf16[16,2,4,128,128]{4,2,3,0,1:T(4,128)(2,1)} fusion(bf16[16,1,4,128,128]{4,2,3,0,1:T(4,128)(2,1)S(1)} %fusion.5, bf16[16,1,4,128,128]{4,2,3,0,1:T(4,128)(2,1)S(1)} %fusion.4), kind=kLoop, calls=%fused_computation.10 | loop fusion | flops 2097152 | bytes 8388608 | tf_op jit(solution)/shard_map/stack | solution.py:59
  55.9 7.7 %gather_fusion.4 = bf16[16,2,4,128,128]{4,2,3,1,0:T(4,128)(2,1)} fusion(bf16[16,2,4,128,128]{4,2,3,0,1:T(4,128)(2,1)} %pad_maximum_fusion, s32[1024]{0:T(1024)S(1)} %pad_clamp_fusion.2), kind=kCustom, calls=%fused_computation.6 | custom fusion | bytes 8388672 | tf_op jit(solution)/shard_map/gather | solution.py:77
  63.5 5.9 %broadcast_select_fusion = bf16[16,2,4,128,128]{4,2,3,1,0:T(4,128)(2,1)} fusion(bf16[16,2,4,128,128]{4,2,3,1,0:T(4,128)(2,1)} %gather_fusion.4, pred[16]{0:T(512)(128)(4,1)S(1)} %fusion.21), kind=kLoop, calls=%fused_computation.16 | loop fusion | flops 2097152 | bytes 8388624 | tf_op jit(solution)/shard_map/jit(_where)/select_n | solution.py:76
  69.5 6.3 %all-to-all-start = ((bf16[16,2,4,128,128]{4,2,3,1,0:T(4,128)(2,1)}), bf16[16,2,4,128,128]{4,2,3,1,0:T(4,128)(2,1)}, u32[]{:S(2)}, u32[]{:S(2)}) async-start(bf16[16,2,4,128,128]{4,2,3,1,0:T(4,128)(2,1)} %broadcast_select_fusion), calls=%async_computation | async-start | bytes 8388608 | tf_op jit(solution)/shard_map/all_to_all | solution.py:79
  75.8 0.1 select_reduce_fusion
  75.9 0.1 reduce_sum.41
  76.0 0.1 reduce_sum.39
  76.1 0.1 reshape.435
  76.2 0.7 gather_fusion.7
  76.9 0.7 gather_fusion.5
  77.7 91.5 %all-to-all-done = bf16[16,2,4,128,128]{4,2,3,1,0:T(4,128)(2,1)} async-done(((bf16[16,2,4,128,128]{4,2,3,1,0:T(4,128)(2,1)}), bf16[16,2,4,128,128]{4,2,3,1,0:T(4,128)(2,1)}, u32[]{:S(2)}, u32[]{:S(2)}) %all-to-all-start) | async-done | bytes 4194336 | tf_op jit(solution)/shard_map/all_to_all | solution.py:79
  169.2 4.9 %bitcast_convert_fusion = bf16[16,4,128,128]{3,2,1,0:T(8,128)(2,1)} fusion(bf16[16,2,4,128,128]{4,2,3,1,0:T(4,128)(2,1)} %all-to-all-done, bf16[16,2,128,128]{3,2,1,0:T(8,128)(2,1)S(1)} %gather_fusion.5, pred[16]{0:T(512)(128)(4,1)S(1)} %compare_and_fusion.2), kind=kOutput, calls=%fused_computation.11 | convolution fusion | flops 538443776 | bytes 7340048 | tf_op jit(solution)/shard_map/nksab,knbc->nsac/dot_general | solution.py:87
  174.1 3.6 %all-to-all-start.1 = ((bf16[16,4,128,128]{3,2,1,0:T(8,128)(2,1)}), bf16[16,4,128,128]{3,2,1,0:T(8,128)(2,1)S(1)}, u32[]{:S(2)}, u32[]{:S(2)}) async-start(bf16[16,4,128,128]{3,2,1,0:T(8,128)(2,1)} %bitcast_convert_fusion), calls=%async_computation.1 | async-start | bytes 4194304 | tf_op jit(solution)/shard_map/all_to_all | solution.py:91
  177.7 0.0 reduce-scatter.2.cloned.1.call-start
  177.7 47.5 %all-to-all-done.1 = bf16[16,4,128,128]{3,2,1,0:T(8,128)(2,1)S(1)} async-done(((bf16[16,4,128,128]{3,2,1,0:T(8,128)(2,1)}), bf16[16,4,128,128]{3,2,1,0:T(8,128)(2,1)S(1)}, u32[]{:S(2)}, u32[]{:S(2)}) %all-to-all-start.1) | async-done | bytes 2097184 | tf_op jit(solution)/shard_map/all_to_all | solution.py:91
  225.3 2.2 gather_fusion.6
  227.4 0.0 reduce-scatter.2.cloned.1.call-update
  227.5 0.1 broadcast_compare_fusion
  227.5 0.2 broadcast_and_fusion.1
  227.8 30.9 %reduce-scatter.2.cloned.1.call-done = bf16[16,4,64,128]{3,2,1,0:T(8,128)(2,1)} async-done(((bf16[16,4,128,128]{3,2,1,0:T(8,128)(2,1)}), bf16[16,4,64,128]{3,2,1,0:T(8,128)(2,1)}) %reduce-scatter.2.cloned.1.call-update) | async-done | bytes 1048592 | tf_op jit(solution)/shard_map/reduce_scatter | solution.py:92
  258.6 2.5 select_convert_fusion
  (27 shorter events, 0.2 us)
Async XLA Ops:
  6.5 70.4 %copy-start = (bf16[2,4,128,128]{3,2,1,0:T(8,128)(2,1)S(1)}, bf16[2,4,128,128]{3,2,1,0:T(8,128)(2,1)}, u32[]{:S(2)}) copy-start(bf16[2,4,128,128]{3,2,1,0:T(8,128)(2,1)} %param.19) | copy-start | bytes 786436
  6.5 10.0 %copy-start.2 = (bf16[16,4,128,128]{3,2,1,0:T(8,128)(2,1)S(1)}, bf16[16,4,128,128]{3,2,1,0:T(8,128)(2,1)}, u32[]{:S(2)}) copy-start(bf16[16,4,128,128]{3,2,1,0:T(8,128)(2,1)} %param.17) | copy-start | bytes 6291460
  28.0 5.3 %copy-start.3 = (f32[2,4,4]{2,1,0:T(4,128)S(1)}, f32[2,4,4]{2,1,0:T(4,128)}, u32[]{:S(2)}) copy-start(f32[2,4,4]{2,1,0:T(4,128)} %param.20) | copy-start | bytes 388
  28.0 5.3 %copy-start.4 = (s32[2,4,4]{2,1,0:T(4,128)S(1)}, s32[2,4,4]{2,1,0:T(4,128)}, u32[]{:S(2)}) copy-start(s32[2,4,4]{2,1,0:T(4,128)} %param.21) | copy-start | bytes 388
  33.3 9.6 %copy-start.1 = (f32[16,4,128,128]{3,1,2,0:T(4,128)S(1)}, f32[16,4,128,128]{3,1,2,0:T(4,128)}, u32[]{:S(2)}) copy-start(f32[16,4,128,128]{3,1,2,0:T(4,128)} %copy.19) | copy-start | bytes 12582916
  69.5 99.7 %all-to-all-start = ((bf16[16,2,4,128,128]{4,2,3,1,0:T(4,128)(2,1)}), bf16[16,2,4,128,128]{4,2,3,1,0:T(4,128)(2,1)}, u32[]{:S(2)}, u32[]{:S(2)}) async-start(bf16[16,2,4,128,128]{4,2,3,1,0:T(4,128)(2,1)} %broadcast_select_fusion), calls=%async_computation | async-start | bytes 8388608 | tf_op jit(solution)/shard_map/all_to_all | solution.py:79
  174.1 51.2 %all-to-all-start.1 = ((bf16[16,4,128,128]{3,2,1,0:T(8,128)(2,1)}), bf16[16,4,128,128]{3,2,1,0:T(8,128)(2,1)S(1)}, u32[]{:S(2)}, u32[]{:S(2)}) async-start(bf16[16,4,128,128]{3,2,1,0:T(8,128)(2,1)} %bitcast_convert_fusion), calls=%async_computation.1 | async-start | bytes 4194304 | tf_op jit(solution)/shard_map/all_to_all | solution.py:91
  177.7 81.0 %reduce-scatter.2.cloned.1.call-start = ((), (), s32[]{:S(2)}) async-start(), calls=%async_computation.3 | async-start | bytes 3145728 | tf_op jit(solution)/shard_map/reduce_scatter | solution.py:92
Sparse Core Ops, SparseCore 0:
  227.6 31.0 reduce-scatter.1
where the time goes:
time: 269 us; the launch traced here: 268 us
  waiting for transfers between devices  170 us (63%)
  local copies, waits for them, and re-layouts  31.3 us (12%)
  matrix products  28 us (10%)
  other arithmetic  15.1 us (6%)
  between operations  13.6 us (5%)
  starting transfers between devices  9.96 us (4%)
    all_to_all x1, waiting for transfers between devices, shards(): lax.all_to_all(outgoing, 'bond', split_axis=0, concat_axis=0, tiled=True)  91.5 us
    all_to_all x1, waiting for transfers between devices, shards(): lax.all_to_all(partial_value, 'bond', split_axis=0, concat_axis=0, tiled=...  47.5 us
    reduce_scatter x1, waiting for transfers between devices, shards(): lax.psum_scatter(returned[back_index].astype(jnp.float32).astype(jnp.bflo...  30.9 us
    dot_general x2, matrix products, shards(): jnp.einsum('st,jtac->jsac', operators[term], product, precision=lax.Preci...  17.5 us
    transpose x2, local copies, waits for them, and re-layouts, shards(): jnp.einsum('jab,jsbc->jsac', chosen, masked, preferred_element_type=jnp.f...  10.5 us
    gather x1, local copies, waits for them, and re-layouts, shards(): mixed[source]  7.67 us
    all_to_all x1, starting transfers between devices, shards(): lax.all_to_all(outgoing, 'bond', split_axis=0, concat_axis=0, tiled=True)  6.32 us
    select_n x1, other arithmetic, shards(): jnp.where(filled[:, None, None, None, None], mixed[source], jnp.zeros((),...  5.9 us
  transfers between devices with their start and end apart: 3, of which 3 were waited for; matrix products, arithmetic and copies ran while one was open for 1% of the time, Pallas kernels for 0%

commit v1 on v0

v1 whole, which is shorter than its diff:
```python
import functools

import jax
import jax.numpy as jnp
from jax import lax
from jax.experimental import pallas as pl
from jax.experimental.pallas import tpu as pltpu
from jax.sharding import PartitionSpec as P

MESH = pl.DeviceIdType.MESH


def loop(count, body):
    if count <= 8:
        for index in range(count):
            body(index)
    else:
        lax.fori_loop(0, count, lambda i, c: (body(i), c)[1], 0)


def kernel(
    sizes,
    psi_ref,
    left_ref,
    right_ref,
    ops_ref,
    pat_ref,
    lmask_ref,
    rmask_ref,
    lsec,
    rsec,
    lsize,
    rsize,
    out_ref,
    psi_v,
    left_v,
    left_all,
    right_own,
    right_oth,
    mix,
    acc,
    out_v,
    ops_all,
    pat_all,
    lmask_all,
    rmask_all,
    coef,
    psi_sem,
    out_sem,
    own_sem,
    small_send,
    small_recv,
    z_send,
    z_recv,
    x_send,
    x_recv,
    cz_send,
    cz_recv,
    cx_send,
    cx_recv,
):
    n_b, n_m, n_p = sizes
    blocks, states, width, _ = psi_ref.shape
    terms = left_ref.shape[0]
    lcount = left_ref.shape[1]
    rcount = right_ref.shape[1]
    rows = width // n_m
    piece = rcount // n_p
    here = lax.axis_index("bond")
    mine = lax.axis_index("mpo")
    lane = lax.axis_index("phys")
    chunks = psi_sem.shape[0]
    per = blocks // chunks

    psi_copies = [
        pltpu.make_async_copy(
            psi_ref.at[pl.ds(c * per, per)], psi_v.at[pl.ds(c * per, per)], psi_sem.at[c]
        )
        for c in range(chunks)
    ]
    own_copies = [
        pltpu.make_async_copy(
            left_ref.at[:, :, pl.ds(mine * rows, rows)], left_v.at[0], own_sem.at[0]
        ),
        pltpu.make_async_copy(
            right_ref, right_own.at[:, pl.ds(here * rcount, rcount)], own_sem.at[1]
        ),
        pltpu.make_async_copy(ops_ref, ops_all.at[0], own_sem.at[2]),
        pltpu.make_async_copy(pat_ref, pat_all.at[0], own_sem.at[3]),
        pltpu.make_async_copy(lmask_ref, lmask_all.at[0], own_sem.at[4]),
        pltpu.make_async_copy(rmask_ref, rmask_all.at[0], own_sem.at[5]),
    ]
    for copy in own_copies + psi_copies:
        copy.start()

    def b_peer(d):
        return lax.rem(here + d, n_b)

    def b_from(d):
        return lax.rem(here + n_b - d, n_b)

    def m_peer(e):
        return lax.rem(mine + e, n_m)

    def p_peer(q):
        return lax.rem(lane + q, n_p)

    barrier = pltpu.get_barrier_semaphore()

    def greet(axis, peer):
        pl.semaphore_signal(barrier, inc=1, device_id={axis: peer}, device_id_type=MESH)

    loop(n_b - 1, lambda i: greet("bond", b_peer(i + 1)))
    loop(n_m - 1, lambda i: greet("mpo", m_peer(i + 1)))
    loop(n_p - 1, lambda i: greet("phys", p_peer(i + 1)))
    pl.semaphore_wait(barrier, n_b + n_m + n_p - 3)

    def remote(src, dst, send, recv, axis, peer):
        return pltpu.make_async_remote_copy(
            src_ref=src,
            dst_ref=dst,
            send_sem=send,
            recv_sem=recv,
            device_id={axis: peer},
            device_id_type=MESH,
        )

    def spot(owner, part):
        return pl.ds(owner * rcount + part * piece, piece)

    def small(e):
        peer = m_peer(e)
        pairs = [
            (ops_ref, ops_all.at[e]),
            (pat_ref, pat_all.at[e]),
            (lmask_ref, lmask_all.at[e]),
            (rmask_ref, rmask_all.at[e]),
            (left_ref.at[:, :, pl.ds(peer * rows, rows)], left_v.at[e]),
        ]
        return [
            remote(s, d, small_send.at[e - 1, i], small_recv.at[e - 1, i], "mpo", peer)
            for i, (s, d) in enumerate(pairs)
        ]

    own_piece = right_ref.at[:, pl.ds(lane * piece, piece)]

    def z_copy(d):
        return remote(
            own_piece,
            right_own.at[:, spot(here, lane)],
            z_send.at[d - 1],
            z_recv.at[d - 1],
            "bond",
            b_peer(d),
        )

    def x_copy(d, e):
        owner = b_from(d)
        src = own_piece if isinstance(d, int) and d == 0 else right_own.at[:, spot(owner, lane)]
        return remote(
            src,
            right_oth.at[e - 1, :, spot(owner, lane)],
            x_send.at[e - 1, d],
            x_recv.at[e - 1, d],
            "mpo",
            m_peer(e),
        )

    def cz_copy(d, q):
        place = right_own.at[:, spot(b_from(d), lane)]
        return remote(
            place, place, cz_send.at[q - 1, d - 1], cz_recv.at[q - 1, d - 1], "phys", p_peer(q)
        )

    def cx_copy(d, e, q):
        place = right_oth.at[e - 1, :, spot(b_from(d), lane)]
        return remote(
            place,
            place,
            cx_send.at[q - 1, e - 1, d],
            cx_recv.at[q - 1, e - 1, d],
            "phys",
            p_peer(q),
        )

    smalls = [c for e in range(1, n_m) for c in small(e)]
    for copy in smalls:
        copy.start()
    for e in range(1, n_m):
        x_copy(0, e).start()
    loop(n_b - 1, lambda i: z_copy(i + 1).start())

    for copy in own_copies:
        copy.wait()
    for copy in smalls:
        copy.wait()

    row_at = mine * rows + lax.broadcasted_iota(jnp.int32, (rows, width), 0)
    col_at = lax.broadcasted_iota(jnp.int32, (rows, width), 1)
    for a in range(lcount):
        size = lsize[here * lcount + a]
        keep = jnp.logical_and(row_at < size, col_at < size)
        for e in range(n_m):
            for k in range(terms):
                on = lmask_all[e, k, here * lcount + a].astype(jnp.float32)
                value = left_v[e, k, a].astype(jnp.float32) * on
                left_all[a, pl.ds((e * terms + k) * rows, rows)] = jnp.where(
                    keep, value, 0.0
                ).astype(jnp.bfloat16)
    for e in range(n_m):
        for k in range(terms):
            for s in range(states):
                for t in range(states):
                    coef[((e * terms + k) * states + s) * states + t] = ops_all[
                        e, k, s, t
                    ] * pat_all[e, k, s, t].astype(jnp.float32)

    base = (here * n_p + lane) * blocks

    def column_keep(b):
        lanes = lax.broadcasted_iota(jnp.int32, (1, width), 1)
        return (lanes < rsize[b]).astype(jnp.float32)

    def left_block(j):
        a = lax.rem(lsec[base + j], lcount)
        b = rsec[base + j]
        keep = column_keep(b).astype(jnp.bfloat16)
        state = jnp.concatenate([psi_v[j, s] * keep for s in range(states)], axis=1)
        for g in range(n_m):
            product = jnp.dot(
                left_all[a, pl.ds(g * terms * rows, terms * rows)],
                state,
                preferred_element_type=jnp.float32,
            )
            for k in range(terms):
                on = rmask_all[g, k, b].astype(jnp.float32)
                at = g * terms + k
                for s in range(states):
                    total = None
                    for t in range(states):
                        weight = coef[(at * states + s) * states + t] * on
                        term = (
                            product[k * rows : (k + 1) * rows, t * width : (t + 1) * width]
                            * weight
                        )
                        total = term if total is None else total + term
                    mix[j, pl.ds(s * rows, rows), pl.ds(at * width, width)] = total.astype(
                        jnp.bfloat16
                    )

    def forward(d):
        z_copy(d).wait_recv()
        for e in range(1, n_m):
            x_copy(d, e).start()
        for q in range(1, n_p):
            cz_copy(d, q).start()

    def forward_x(d):
        for e in range(1, n_m):
            x_copy(d, e).wait_recv()
            for q in range(1, n_p):
                cx_copy(d, e, q).start()

    def left_chunk(c):
        psi_copies[c].wait()
        lax.fori_loop(c * per, (c + 1) * per, lambda j, carry: (left_block(j), carry)[1], 0, unroll=2)

    for c in range(chunks):
        left_chunk(c)
        if n_b <= 8 and c < n_b - 1:
            forward(c + 1)
    if n_b <= 8:
        for d in range(chunks + 1, n_b):
            forward(d)
    else:
        lax.fori_loop(1, n_b, lambda d, carry: (forward(d), carry)[1], 0)

    forward_x(0)

    def own_ready(d):
        for q in range(1, n_p):
            cz_copy(d, q).wait()

    loop(n_b - 1, lambda i: own_ready(i + 1))

    def right_own_block(j, carry):
        b = rsec[base + j]
        weights = jnp.concatenate([right_own[k, b] for k in range(terms)], axis=0)
        acc[j] = jnp.dot(
            mix[j, :, pl.ds(0, terms * width)], weights, preferred_element_type=jnp.float32
        )
        return carry

    lax.fori_loop(0, blocks, right_own_block, 0, unroll=2)

    loop(n_b - 1, lambda i: forward_x(i + 1))

    def oth_ready(d):
        for e in range(1, n_m):
            for q in range(1, n_p):
                cx_copy(d, e, q).wait()

    loop(n_b, oth_ready)

    def out_copy(j):
        return pltpu.make_async_copy(out_v.at[j], out_ref.at[j], out_sem.at[j])

    def right_oth_block(j, carry):
        b = rsec[base + j]
        total = acc[j]
        for e in range(1, n_m):
            weights = jnp.concatenate([right_oth[e - 1, k, b] for k in range(terms)], axis=0)
            total = total + jnp.dot(
                mix[j, :, pl.ds(e * terms * width, terms * width)],
                weights,
                preferred_element_type=jnp.float32,
            )
        total = (total * column_keep(b)).astype(jnp.bfloat16)
        for s in range(states):
            out_v[j, s] = total[s * rows : (s + 1) * rows]
        out_copy(j).start()
        return carry

    lax.fori_loop(0, blocks, right_oth_block, 0, unroll=2)

    def sent(d):
        z_copy(d).wait_send()

    loop(n_b - 1, lambda i: sent(i + 1))

    def sent_x(d):
        for e in range(1, n_m):
            x_copy(d, e).wait_send()

    loop(n_b, sent_x)
    lax.fori_loop(0, blocks, lambda j, carry: (out_copy(j).wait(), carry)[1], 0)


def shards(
    psi,
    left_env,
    right_env,
    mpo_ops,
    mpo_pattern,
    left_mask,
    right_mask,
    left_sector,
    right_sector,
    left_size,
    right_size,
):
    blocks, states, width, _ = psi.shape
    terms, lcount = left_env.shape[:2]
    rcount = right_env.shape[1]
    n_b, n_m, n_p = (lax.axis_size(a) for a in ("bond", "mpo", "phys"))
    rows = width // n_m
    sectors = n_b * rcount
    lefts = left_size.shape[0]
    bf16, f32, i32 = jnp.bfloat16, jnp.float32, jnp.int32
    chunks = 4
    dma = pltpu.SemaphoreType.DMA
    anyspace = pl.BlockSpec(memory_space=pl.ANY)
    smem = pl.BlockSpec(memory_space=pltpu.SMEM)
    return pl.pallas_call(
        functools.partial(kernel, (n_b, n_m, n_p)),
        out_shape=jax.ShapeDtypeStruct((blocks, states, rows, width), bf16),
        in_specs=[anyspace] * 7 + [smem] * 4,
        out_specs=anyspace,
        scratch_shapes=[
            pltpu.VMEM((blocks, states, width, width), bf16),
            pltpu.VMEM((n_m, terms, lcount, rows, width), bf16),
            pltpu.VMEM((lcount, n_m * terms * rows, width), bf16),
            pltpu.VMEM((terms, sectors, width, width), bf16),
            pltpu.VMEM((n_m - 1, terms, sectors, width, width), bf16),
            pltpu.VMEM((blocks, states * rows, n_m * terms * width), bf16),
            pltpu.VMEM((blocks, states * rows, width), f32),
            pltpu.VMEM((blocks, states, rows, width), bf16),
            pltpu.SMEM((n_m, terms, states, states), f32),
            pltpu.SMEM((n_m, terms, states, states), i32),
            pltpu.SMEM((n_m, terms, lefts), i32),
            pltpu.SMEM((n_m, terms, sectors), i32),
            pltpu.SMEM((n_m * terms * states * states,), f32),
            dma((chunks,)),
            dma((blocks,)),
            dma((6,)),
            dma((n_m - 1, 5)),
            dma((n_m - 1, 5)),
            dma((n_b - 1,)),
            dma((n_b - 1,)),
            dma((n_m - 1, n_b)),
            dma((n_m - 1, n_b)),
            dma((n_p - 1, n_b - 1)),
            dma((n_p - 1, n_b - 1)),
            dma((n_p - 1, n_m - 1, n_b)),
            dma((n_p - 1, n_m - 1, n_b)),
        ],
        compiler_params=pltpu.CompilerParams(
            collective_id=0, has_side_effects=True, vmem_limit_bytes=56 * 1024 * 1024
        ),
    )(
        psi,
        left_env,
        right_env,
        mpo_ops,
        mpo_pattern,
        left_mask,
        right_mask,
        left_sector,
        right_sector,
        left_size,
        right_size,
    )


def solution(mesh):
    placed = (
        P(("groups", "bond", "phys"), None, None, None),
        P("mpo", ("groups", "bond"), None, None),
        P("mpo", ("groups", "bond"), None, None),
        P("mpo", None, None),
        P("mpo", None, None),
        P("mpo", "groups"),
        P("mpo", "groups"),
        P("groups"),
        P("groups"),
        P("groups"),
        P("groups"),
    )
    return jax.shard_map(
        shards,
        mesh=mesh,
        in_specs=placed,
        out_specs=P(("groups", "bond", "phys"), None, "mpo", None),
        check_vma=False,
    )
```

time: 269 us -> 29.6 us (0.11)
  waiting for transfers between devices: 170 us -> 0 us
  local copies, waits for them, and re-layouts: 31.3 us -> 2.29 us
  matrix products: 28 us -> 0 us
  Pallas kernels: 0 us -> 27.1 us
  other arithmetic: 15.1 us -> 0 us
  between operations: 13.6 us -> 0.01 us
  starting transfers between devices: 9.96 us -> 0 us
    all_to_all x2 -> x0, waiting for transfers between devices: 139 us -> none  [the longest x1 91.5 us: shards(): lax.all_to_all(outgoing, 'bond', split_axis=0, concat_axis=0, tiled=True)]
    reduce_scatter x1 -> x0, waiting for transfers between devices: 30.9 us -> none  [shards(): lax.psum_scatter(returned[back_index].astype(jnp.float32).astype(jnp.bflo...]
    dot_general x5 -> x0, matrix products: 28 us -> none  [the longest x2 17.5 us: shards(): jnp.einsum('st,jtac->jsac', operators[term], product, precision=lax.Preci...]
    pallas_call x0 -> x1, Pallas kernels: none -> 27.1 us  [shards(): pl.pallas_call(functools.partial(kernel, (n_b, n_m, n_p)), out_shape=jax....]
    gather x11 -> x0, local copies, waits for them, and re-layouts: 16.4 us -> none  [the longest x1 7.67 us: shards(): mixed[source]]
    transpose x2 -> x0, local copies, waits for them, and re-layouts: 10.5 us -> none  [shards(): jnp.einsum('jab,jsbc->jsac', chosen, masked, preferred_element_type=jnp.f...]
    all_to_all x2 -> x0, starting transfers between devices: 9.92 us -> none  [the longest x1 6.32 us: shards(): lax.all_to_all(outgoing, 'bond', split_axis=0, concat_axis=0, tiled=True)]
    select_n x7 -> x0, other arithmetic: 5.96 us -> none  [the longest x1 5.9 us: shards(): jnp.where(filled[:, None, None, None, None], mixed[source], jnp.zeros((),...]
  transfers between devices with their start and end apart: 3 -> 0, of which waited for: 3 -> 0; matrix products, arithmetic and copies ran while one was open for 1% -> 0% of each run, Pallas kernels for 0% -> 0%
where the time goes in v1:
time: 29.6 us; the launch traced here: 29.4 us
  Pallas kernels  27.1 us (92%)
  local copies, waits for them, and re-layouts  2.29 us (8%)
    pallas_call x1, Pallas kernels, shards(): pl.pallas_call(functools.partial(kernel, (n_b, n_m, n_p)), out_shape=jax....  27.1 us
    unnamed x1, local copies, waits for them, and re-layouts  2.29 us

profile of v1, /device:TPU:0, one launch (start us, length us, event | category | flops | bytes accessed | tf_op | source)
XLA Modules:
  0.0 29.4 jit_solution(15979555696296092570)
XLA Ops:
  0.0 27.1 %shard_map.109 = bf16[16,4,64,128]{3,2,1,0:T(8,128)(2,1)} custom-call(bf16[16,4,128,128]{3,2,1,0:T(8,128)(2,1)} %psi_ref.1, bf16[2,2,128,128]{3,2,1,0:T(8,128)(2,1)} %left_ref.1, bf16[2,4,128,128]{3,2,1,0:T(8,128)(2,1)} %right_ref.1, f32[2,4,4]{2,1,0:T(4,128)} %ops_ref.1, s32[2,4,4]{2,1,0:T(4,128)} %pat_ref.1, s32[2,8]{1,0:T(2,128)} %lmask_ref.1, ...), custom_call_target="tpu_custom_call" | custom-call | tf_op jit(solution)/shard_map/pallas_call | solution.py:364
  27.1 2.3 %copy.13 = bf16[16,4,64,128]{3,2,1,0:T(8,128)(2,1)} copy(bf16[16,4,64,128]{3,2,1,0:T(8,128)(2,1)} %shard_map.109) | data formatting | bytes 2097152

commit v2 on v1

--- a/solution.py
+++ b/solution.py
@@ -27,16 +27,15 @@
     pat_ref,
     lmask_ref,
     rmask_ref,
-    lsec,
-    rsec,
-    lsize,
-    rsize,
+    lsec_ref,
+    rsec_ref,
+    lsize_ref,
+    rsize_ref,
     out_ref,
     psi_v,
     left_v,
     left_all,
     right_own,
-    right_oth,
     mix,
     acc,
     out_v,
@@ -45,6 +44,10 @@
     lmask_all,
     rmask_all,
     coef,
+    lsec,
+    rsec,
+    lsize,
+    rsize,
     psi_sem,
     out_sem,
     own_sem,
@@ -58,6 +61,7 @@
     cz_recv,
     cx_send,
     cx_recv,
+    *right_oth,
 ):
     n_b, n_m, n_p = sizes
     blocks, states, width, _ = psi_ref.shape
@@ -89,14 +93,21 @@
         pltpu.make_async_copy(pat_ref, pat_all.at[0], own_sem.at[3]),
         pltpu.make_async_copy(lmask_ref, lmask_all.at[0], own_sem.at[4]),
         pltpu.make_async_copy(rmask_ref, rmask_all.at[0], own_sem.at[5]),
+        pltpu.make_async_copy(lsec_ref, lsec, own_sem.at[6]),
+        pltpu.make_async_copy(rsec_ref, rsec, own_sem.at[7]),
+        pltpu.make_async_copy(lsize_ref, lsize, own_sem.at[8]),
+        pltpu.make_async_copy(rsize_ref, rsize, own_sem.at[9]),
     ]
-    for copy in own_copies + psi_copies:
-        copy.start()
+    line = n_b == 4
 
     def b_peer(d):
+        if line:
+            return (here, here + 1 - 2 * lax.rem(here, 2), lax.rem(here + 2, 4), 3 - here)[d]
         return lax.rem(here + d, n_b)
 
     def b_from(d):
+        if line:
+            return b_peer(d)
         return lax.rem(here + n_b - d, n_b)
 
     def m_peer(e):
@@ -113,6 +124,8 @@
     loop(n_b - 1, lambda i: greet("bond", b_peer(i + 1)))
     loop(n_m - 1, lambda i: greet("mpo", m_peer(i + 1)))
     loop(n_p - 1, lambda i: greet("phys", p_peer(i + 1)))
+    for copy in own_copies + psi_copies:
+        copy.start()
     pl.semaphore_wait(barrier, n_b + n_m + n_p - 3)
 
     def remote(src, dst, send, recv, axis, peer):
@@ -142,53 +155,79 @@
             for i, (s, d) in enumerate(pairs)
         ]
 
-    own_piece = right_ref.at[:, pl.ds(lane * piece, piece)]
-
-    def z_copy(d):
+    def own_piece(t):
+        return right_ref.at[t, pl.ds(lane * piece, piece)]
+
+    def z_copy(d, t):
         return remote(
-            own_piece,
-            right_own.at[:, spot(here, lane)],
-            z_send.at[d - 1],
-            z_recv.at[d - 1],
+            own_piece(t),
+            right_own.at[t, spot(here, lane)],
+            z_send.at[d - 1, t],
+            z_recv.at[d - 1, t],
             "bond",
             b_peer(d),
         )
 
-    def x_copy(d, e):
+    def z_relay(t):
+        place = right_own.at[t, spot(b_from(3), lane)]
+        return remote(place, place, z_send.at[1, t], z_recv.at[1, t], "bond", b_peer(1))
+
+    def x_copy(d, e, t):
         owner = b_from(d)
-        src = own_piece if isinstance(d, int) and d == 0 else right_own.at[:, spot(owner, lane)]
+        own = isinstance(d, int) and d == 0
+        src = own_piece(t) if own else right_own.at[t, spot(owner, lane)]
         return remote(
             src,
-            right_oth.at[e - 1, :, spot(owner, lane)],
-            x_send.at[e - 1, d],
-            x_recv.at[e - 1, d],
+            right_oth[t].at[e - 1, spot(owner, lane)],
+            x_send.at[e - 1, d, t],
+            x_recv.at[e - 1, d, t],
             "mpo",
             m_peer(e),
         )
 
-    def cz_copy(d, q):
-        place = right_own.at[:, spot(b_from(d), lane)]
-        return remote(
-            place, place, cz_send.at[q - 1, d - 1], cz_recv.at[q - 1, d - 1], "phys", p_peer(q)
-        )
-
-    def cx_copy(d, e, q):
-        place = right_oth.at[e - 1, :, spot(b_from(d), lane)]
+    def cz_copy(d, q, t):
+        place = right_own.at[t, spot(b_from(d), lane)]
         return remote(
             place,
             place,
-            cx_send.at[q - 1, e - 1, d],
-            cx_recv.at[q - 1, e - 1, d],
+            cz_send.at[q - 1, d - 1, t],
+            cz_recv.at[q - 1, d - 1, t],
             "phys",
             p_peer(q),
         )
 
+    def cx_copy(d, e, q, t):
+        place = right_oth[t].at[e - 1, spot(b_from(d), lane)]
+        return remote(
+            place,
+            place,
+            cx_send.at[q - 1, e - 1, d, t],
+            cx_recv.at[q - 1, e - 1, d, t],
+            "phys",
+            p_peer(q),
+        )
+
     smalls = [c for e in range(1, n_m) for c in small(e)]
+    middle = jnp.logical_and(here > 0, here < n_b - 1)
     for copy in smalls:
         copy.start()
-    for e in range(1, n_m):
-        x_copy(0, e).start()
-    loop(n_b - 1, lambda i: z_copy(i + 1).start())
+    for t in range(terms):
+        for e in range(1, n_m):
+            x_copy(0, e, t).start()
+        if line:
+
+            def send_middle(t=t):
+                z_copy(3, t).start()
+                z_copy(1, t).start()
+
+            def send_end(t=t):
+                for d in (1, 2, 3):
+                    z_copy(d, t).start()
+
+            pl.when(middle)(send_middle)
+            pl.when(jnp.logical_not(middle))(send_end)
+        else:
+            loop(n_b - 1, lambda i, t=t: z_copy(i + 1, t).start())
 
     for copy in own_copies:
         copy.wait()
@@ -248,38 +287,59 @@
                         jnp.bfloat16
                     )
 
-    def forward(d):
-        z_copy(d).wait_recv()
+    def forward(d, t):
+        z_copy(d, t).wait_recv()
+        if line and d == 3:
+            pl.when(middle)(lambda: z_relay(t).start())
         for e in range(1, n_m):
-            x_copy(d, e).start()
+            x_copy(d, e, t).start()
         for q in range(1, n_p):
-            cz_copy(d, q).start()
-
-    def forward_x(d):
+            cz_copy(d, q, t).start()
+
+    def forward_x(d, t):
         for e in range(1, n_m):
-            x_copy(d, e).wait_recv()
+            x_copy(d, e, t).wait_recv()
             for q in range(1, n_p):
-                cx_copy(d, e, q).start()
+                cx_copy(d, e, q, t).start()
 
     def left_chunk(c):
         psi_copies[c].wait()
         lax.fori_loop(c * per, (c + 1) * per, lambda j, carry: (left_block(j), carry)[1], 0, unroll=2)
 
+    if line:
+        steps = [lambda d=d, t=t: forward(d, t) for t in range(terms) for d in (1, 3, 2)]
+    else:
+        steps = [
+            lambda t=t: loop(n_b - 1, lambda i: forward(i + 1, t)) for t in range(terms)
+        ]
     for c in range(chunks):
         left_chunk(c)
-        if n_b <= 8 and c < n_b - 1:
-            forward(c + 1)
-    if n_b <= 8:
-        for d in range(chunks + 1, n_b):
-            forward(d)
-    else:
-        lax.fori_loop(1, n_b, lambda d, carry: (forward(d), carry)[1], 0)
-
-    forward_x(0)
+        if steps:
+            steps.pop(0)()
+    for t in range(terms):
+        forward_x(0, t)
+    for step in steps:
+        step()
 
     def own_ready(d):
         for q in range(1, n_p):
-            cz_copy(d, q).wait()
+            for t in range(terms):
+                cz_copy(d, q, t).wait()
+
+    def oth_forward(t):
+        if line:
+            for d in (1, 3, 2):
+                forward_x(d, t)
+        else:
+            loop(n_b - 1, lambda i: forward_x(i + 1, t))
+
+    def oth_ready(t):
+        def one(d):
+            for e in range(1, n_m):
+                for q in range(1, n_p):
+                    cx_copy(d, e, q, t).wait()
+
+        loop(n_b, one)
 
     loop(n_b - 1, lambda i: own_ready(i + 1))
 
@@ -293,44 +353,46 @@
 
     lax.fori_loop(0, blocks, right_own_block, 0, unroll=2)
 
-    loop(n_b - 1, lambda i: forward_x(i + 1))
-
-    def oth_ready(d):
-        for e in range(1, n_m):
-            for q in range(1, n_p):
-                cx_copy(d, e, q).wait()
-
-    loop(n_b, oth_ready)
-
     def out_copy(j):
         return pltpu.make_async_copy(out_v.at[j], out_ref.at[j], out_sem.at[j])
 
-    def right_oth_block(j, carry):
-        b = rsec[base + j]
+    def oth_total(j, b, t):
         total = acc[j]
         for e in range(1, n_m):
-            weights = jnp.concatenate([right_oth[e - 1, k, b] for k in range(terms)], axis=0)
             total = total + jnp.dot(
-                mix[j, :, pl.ds(e * terms * width, terms * width)],
-                weights,
+                mix[j, :, pl.ds((e * terms + t) * width, width)],
+                right_oth[t][e - 1, b],
                 preferred_element_type=jnp.float32,
             )
+        return total
+
+    def right_oth_block(t, j, carry):
+        b = rsec[base + j]
+        total = oth_total(j, b, t)
+        if t < terms - 1:
+            acc[j] = total
+            return carry
         total = (total * column_keep(b)).astype(jnp.bfloat16)
         for s in range(states):
             out_v[j, s] = total[s * rows : (s + 1) * rows]
         out_copy(j).start()
         return carry
 
-    lax.fori_loop(0, blocks, right_oth_block, 0, unroll=2)
+    for t in range(terms):
+        oth_forward(t)
+        oth_ready(t)
+        lax.fori_loop(0, blocks, functools.partial(right_oth_block, t), 0, unroll=2)
 
     def sent(d):
-        z_copy(d).wait_send()
+        for t in range(terms):
+            z_copy(d, t).wait_send()
 
     loop(n_b - 1, lambda i: sent(i + 1))
 
     def sent_x(d):
-        for e in range(1, n_m):
-            x_copy(d, e).wait_send()
+        for t in range(terms):
+            for e in range(1, n_m):
+                x_copy(d, e, t).wait_send()
 
     loop(n_b, sent_x)
     lax.fori_loop(0, blocks, lambda j, carry: (out_copy(j).wait(), carry)[1], 0)
@@ -360,18 +422,16 @@
     chunks = 4
     dma = pltpu.SemaphoreType.DMA
     anyspace = pl.BlockSpec(memory_space=pl.ANY)
-    smem = pl.BlockSpec(memory_space=pltpu.SMEM)
     return pl.pallas_call(
         functools.partial(kernel, (n_b, n_m, n_p)),
         out_shape=jax.ShapeDtypeStruct((blocks, states, rows, width), bf16),
-        in_specs=[anyspace] * 7 + [smem] * 4,
+        in_specs=[anyspace] * 11,
         out_specs=anyspace,
         scratch_shapes=[
             pltpu.VMEM((blocks, states, width, width), bf16),
             pltpu.VMEM((n_m, terms, lcount, rows, width), bf16),
             pltpu.VMEM((lcount, n_m * terms * rows, width), bf16),
             pltpu.VMEM((terms, sectors, width, width), bf16),
-            pltpu.VMEM((n_m - 1, terms, sectors, width, width), bf16),
             pltpu.VMEM((blocks, states * rows, n_m * terms * width), bf16),
             pltpu.VMEM((blocks, states * rows, width), f32),
             pltpu.VMEM((blocks, states, rows, width), bf16),
@@ -380,20 +440,25 @@
             pltpu.SMEM((n_m, terms, lefts), i32),
             pltpu.SMEM((n_m, terms, sectors), i32),
             pltpu.SMEM((n_m * terms * states * states,), f32),
+            pltpu.SMEM(left_sector.shape, i32),
+            pltpu.SMEM(right_sector.shape, i32),
+            pltpu.SMEM(left_size.shape, i32),
+            pltpu.SMEM(right_size.shape, i32),
             dma((chunks,)),
             dma((blocks,)),
-            dma((6,)),
+            dma((10,)),
             dma((n_m - 1, 5)),
             dma((n_m - 1, 5)),
-            dma((n_b - 1,)),
-            dma((n_b - 1,)),
-            dma((n_m - 1, n_b)),
-            dma((n_m - 1, n_b)),
-            dma((n_p - 1, n_b - 1)),
-            dma((n_p - 1, n_b - 1)),
-            dma((n_p - 1, n_m - 1, n_b)),
-            dma((n_p - 1, n_m - 1, n_b)),
-        ],
+            dma((n_b - 1, terms)),
+            dma((n_b - 1, terms)),
+            dma((n_m - 1, n_b, terms)),
+            dma((n_m - 1, n_b, terms)),
+            dma((n_p - 1, n_b - 1, terms)),
+            dma((n_p - 1, n_b - 1, terms)),
+            dma((n_p - 1, n_m - 1, n_b, terms)),
+            dma((n_p - 1, n_m - 1, n_b, terms)),
+        ]
+        + [pltpu.VMEM((n_m - 1, sectors, width, width), bf16) for _ in range(terms)],
         compiler_params=pltpu.CompilerParams(
             collective_id=0, has_side_effects=True, vmem_limit_bytes=56 * 1024 * 1024
         ),

time: 29.6 us -> 29.3 us (0.990)
  Pallas kernels: 27.1 us -> 26.8 us
    pallas_call x1, Pallas kernels: 27.1 us -> 26.8 us  [shards(): pl.pallas_call(functools.partial(kernel, (n_b, n_m, n_p)), out_shape=jax....]
where the time goes in v2:
time: 29.3 us; the launch traced here: 29.1 us
  Pallas kernels  26.8 us (91%)
  local copies, waits for them, and re-layouts  2.29 us (8%)
    pallas_call x1, Pallas kernels, shards(): pl.pallas_call(functools.partial(kernel, (n_b, n_m, n_p)), out_shape=jax....  26.8 us
    unnamed x1, local copies, waits for them, and re-layouts  2.29 us

profile of v2, /device:TPU:0, one launch (start us, length us, event | category | flops | bytes accessed | tf_op | source)
XLA Modules:
  0.0 29.1 jit_solution(11103868238190003844)
XLA Ops:
  0.0 26.8 %shard_map.109 = bf16[16,4,64,128]{3,2,1,0:T(8,128)(2,1)} custom-call(bf16[16,4,128,128]{3,2,1,0:T(8,128)(2,1)} %psi_ref.1, bf16[2,2,128,128]{3,2,1,0:T(8,128)(2,1)} %left_ref.1, bf16[2,4,128,128]{3,2,1,0:T(8,128)(2,1)} %right_ref.1, f32[2,4,4]{2,1,0:T(4,128)} %ops_ref.1, s32[2,4,4]{2,1,0:T(4,128)} %pat_ref.1, s32[2,8]{1,0:T(2,128)} %lmask_ref.1, ...), custom_call_target="tpu_custom_call" | custom-call | tf_op jit(solution)/shard_map/pallas_call | solution.py:425
  26.8 2.3 %copy.13 = bf16[16,4,64,128]{3,2,1,0:T(8,128)(2,1)} copy(bf16[16,4,64,128]{3,2,1,0:T(8,128)(2,1)} %shard_map.109) | data formatting | bytes 2097152

commit v3 on v2

--- a/solution.py
+++ b/solution.py
@@ -341,6 +341,7 @@
 
         loop(n_b, one)
 
+    oth_forward(0)
     loop(n_b - 1, lambda i: own_ready(i + 1))
 
     def right_own_block(j, carry):
@@ -351,7 +352,7 @@
         )
         return carry
 
-    lax.fori_loop(0, blocks, right_own_block, 0, unroll=2)
+    lax.fori_loop(0, blocks, right_own_block, 0, unroll=4)
 
     def out_copy(j):
         return pltpu.make_async_copy(out_v.at[j], out_ref.at[j], out_sem.at[j])
@@ -379,9 +380,10 @@
         return carry
 
     for t in range(terms):
-        oth_forward(t)
+        if t > 0:
+            oth_forward(t)
         oth_ready(t)
-        lax.fori_loop(0, blocks, functools.partial(right_oth_block, t), 0, unroll=2)
+        lax.fori_loop(0, blocks, functools.partial(right_oth_block, t), 0, unroll=4)
 
     def sent(d):
         for t in range(terms):
@@ -396,6 +398,29 @@
 
     loop(n_b, sent_x)
     lax.fori_loop(0, blocks, lambda j, carry: (out_copy(j).wait(), carry)[1], 0)
+
+
+def place(parts, src, dst, buf, sem, sem2):
+    step = src.shape[0] // parts
+    ins = [
+        pltpu.make_async_copy(
+            src.at[pl.ds(c * step, step)], buf.at[pl.ds(c * step, step)], sem.at[c]
+        )
+        for c in range(parts)
+    ]
+    outs = [
+        pltpu.make_async_copy(
+            buf.at[pl.ds(c * step, step)], dst.at[pl.ds(c * step, step)], sem2.at[c]
+        )
+        for c in range(parts)
+    ]
+    for copy in ins:
+        copy.start()
+    for a, b in zip(ins, outs):
+        a.wait()
+        b.start()
+    for copy in outs:
+        copy.wait()
 
 
 def shards(
@@ -422,7 +447,7 @@
     chunks = 4
     dma = pltpu.SemaphoreType.DMA
     anyspace = pl.BlockSpec(memory_space=pl.ANY)
-    return pl.pallas_call(
+    h = pl.pallas_call(
         functools.partial(kernel, (n_b, n_m, n_p)),
         out_shape=jax.ShapeDtypeStruct((blocks, states, rows, width), bf16),
         in_specs=[anyspace] * 11,
@@ -475,6 +500,13 @@
         left_size,
         right_size,
     )
+    return pl.pallas_call(
+        functools.partial(place, 8),
+        out_shape=jax.ShapeDtypeStruct(h.shape, h.dtype),
+        in_specs=[anyspace],
+        out_specs=anyspace,
+        scratch_shapes=[pltpu.VMEM(h.shape, h.dtype), dma((8,)), dma((8,))],
+    )(h)
 
 
 def solution(mesh):

time: 29.3 us -> 27.5 us (0.939)
  local copies, waits for them, and re-layouts: 2.29 us -> 0 us
  Pallas kernels: 26.8 us -> 27.4 us
    unnamed x1 -> x0, local copies, waits for them, and re-layouts: 2.29 us -> none
    pallas_call x0 -> x1, Pallas kernels: none -> 2.09 us  [shards(): pl.pallas_call(functools.partial(place, 8), out_shape=jax.ShapeDtypeStruc...]
    pallas_call x1, Pallas kernels: 26.8 us -> 25.3 us  [shards(): pl.pallas_call(functools.partial(kernel, (n_b, n_m, n_p)), out_shape=jax....]
where the time goes in v3:
time: 27.5 us; the launch traced here: 27.4 us
  Pallas kernels  27.4 us (100%)
    pallas_call x1, Pallas kernels, shards(): pl.pallas_call(functools.partial(kernel, (n_b, n_m, n_p)), out_shape=jax....  25.3 us
    pallas_call x1, Pallas kernels, shards(): pl.pallas_call(functools.partial(place, 8), out_shape=jax.ShapeDtypeStruc...  2.09 us

profile of v3, /device:TPU:0, one launch (start us, length us, event | category | flops | bytes accessed | tf_op | source)
XLA Modules:
  0.0 27.4 jit_solution(5947804019648623095)
XLA Ops:
  0.0 25.3 %shard_map.109.src = bf16[16,4,64,128]{3,2,1,0:T(8,128)(2,1)} custom-call(bf16[16,4,128,128]{3,2,1,0:T(8,128)(2,1)} %psi_ref.1, bf16[2,2,128,128]{3,2,1,0:T(8,128)(2,1)} %left_ref.1, bf16[2,4,128,128]{3,2,1,0:T(8,128)(2,1)} %right_ref.1, f32[2,4,4]{2,1,0:T(4,128)} %ops_ref.1, s32[2,4,4]{2,1,0:T(4,128)} %pat_ref.1, s32[2,8]{1,0:T(2,128)} %lmask_ref.1, ...), custom_call_target="tpu_custom_call" | custom-call | tf_op jit(solution)/shard_map/pallas_call | solution.py:450
  25.3 2.1 %shard_map.110 = bf16[16,4,64,128]{3,2,1,0:T(8,128)(2,1)} custom-call(bf16[16,4,64,128]{3,2,1,0:T(8,128)(2,1)} %shard_map.109.src), custom_call_target="tpu_custom_call" | custom-call | tf_op jit(solution)/shard_map/pallas_call | solution.py:503
